TPU v7x, 32 devices: a whole 2x2x4 slice. The times are simulated.
32 devices in a mesh: groups: 2 (over y), orient: 4 (over z), img: 2 (over x), brick: 2 (over core).
Axes of the slice: x: 2, y: 2, z: 4, core: 2. Of those that a mesh axis runs over, the one named last changes fastest.
Arguments:
- images: bfloat16 [1024, 4096], P(('groups', 'orient', 'img', 'brick')), parts along dimension 0, may hold values from -8 to 8
- offsets: int32 [1024, 2], P('groups'), parts along dimension 0, may hold values from -6 to 6
- slices: bfloat16 [2048, 4096], P(('groups', 'orient')), parts along dimension 0, may hold values from -3 to 3
- seg_map: int32 [8192, 1], replicated, may hold values from 0 to 15; in each aligned block of 512 rows (0 to 511, 512 to 1023, ...) at most 64 rows name the same one
- interp: int32 [16, 8, 256, 256], P(('orient', 'img', 'brick')), may hold values from 0 to 4095
Outputs:
- brick_values: float32 [32, 2, 256], P(('groups', 'orient', 'img', 'brick')), parts along dimension 0
- brick_weight: float32 [32, 256], P(('groups', 'orient', 'img', 'brick')), parts along dimension 0
There are 2 independent parts, one for each index of `groups`. A program takes and returns all parts, laid end to end along the dimension named above; an argument that names none is the same for every part. Nothing has to cross between parts.
Inputs may be any that keep to these rules, and one draw needn't show every extreme that they name: `seg_map`: in each aligned block of 512 rows no brick is named by more than 64 rows; in every draw some block names some brick exactly 64 times.
All inputs are finite; a program needn't handle non-finite values.
Results may differ from a plain program's by a relative error of at most 0.019.
Values may be sent and summed in bfloat16 or wider, within the bound.
A program may use at most 64 MiB of HBM per device.

v0:
```python
import jax
import jax.numpy as jnp
from jax import lax
from jax.sharding import PartitionSpec as P

K = 2048
SHIFTS = 16
SEG = 256


frame_side = 64
interp_scale = 1.0 / 256.0


def combined_all(array, axis, combine):
    everything = jax.tree.map(lambda part: lax.all_gather(part, axis), array)
    leading = jax.tree.map(lambda part: part[0], everything)

    def turn(k, so_far):
        return combine(so_far, jax.tree.map(lambda part: part[k], everything))

    return lax.fori_loop(1, lax.axis_size(axis), turn, leading)


def shift_images(image_rows, image_offsets):
    row_count = image_rows.shape[0]
    coeffs = image_rows.shape[1] // 2
    coef_index = jnp.arange(coeffs, dtype=jnp.int32)
    column_freq = coef_index % frame_side - frame_side // 2
    row_freq = coef_index // frame_side
    shift_index = jnp.arange(SHIFTS, dtype=jnp.int32)
    shift_x = image_offsets[:, 0][:, None] + (shift_index % 4 - 2)[None, :]
    shift_y = image_offsets[:, 1][:, None] + (shift_index // 4 - 2)[None, :]
    phase_index = jnp.mod(
        shift_x[:, :, None] * column_freq[None, None, :]
        + shift_y[:, :, None] * row_freq[None, None, :],
        frame_side,
    )
    angle = phase_index.astype(jnp.float32) * (2.0 * jnp.pi / frame_side)
    cosine = jnp.cos(angle)
    sine = jnp.sin(angle)
    real_part = image_rows[:, :coeffs].astype(jnp.float32)[:, None, :]
    imag_part = image_rows[:, coeffs:].astype(jnp.float32)[:, None, :]
    out_real = real_part * cosine + imag_part * sine
    out_imag = imag_part * cosine - real_part * sine
    joined = jnp.concatenate([out_real, out_imag], axis=-1).astype(jnp.bfloat16)
    return joined.reshape(row_count * SHIFTS, 2 * coeffs)


def combine_mass(first, second):
    top_score = jnp.maximum(first[0], second[0])
    return (
        top_score,
        first[1] * jnp.exp(first[0] - top_score) + second[1] * jnp.exp(second[0] - top_score),
    )


def per_device(images, offsets, slices, seg_map, interp):
    inv_noise = 100.0 / K
    orient_count = lax.axis_size("orient")
    group_count = lax.axis_size("img") * lax.axis_size("brick")
    group_index = lax.axis_index("img") * lax.axis_size("brick") + lax.axis_index("brick")
    flat_index = lax.axis_index("orient") * group_count + group_index
    brick_count = orient_count * group_count
    per_shard = images.shape[0]
    orient_local = slices.shape[0]
    group_offsets = lax.dynamic_index_in_dim(
        offsets.reshape(orient_count, group_count, per_shard, 2), group_index, 1, keepdims=False
    )
    group_offsets = group_offsets.reshape(orient_count * per_shard, 2)
    shifted = shift_images(lax.all_gather(images, "orient", axis=0, tiled=True), group_offsets)
    half_norm = 0.5 * jnp.sum(jnp.square(slices.astype(jnp.float32)), axis=1)
    intersections = lax.dot_general(
        shifted, slices, (((1,), (1,)), ((), ())), preferred_element_type=jnp.float32
    )
    score = inv_noise * (intersections - half_norm[None, :])
    per_image = score.reshape(-1, SHIFTS * orient_local)
    local_top = jnp.max(per_image, axis=1)
    local_terms = jnp.exp(per_image - local_top[:, None])
    local_mass = jnp.sum(local_terms, axis=1)
    top_score, mass_total = combined_all((local_top, local_mass), "orient", combine_mass)
    exp_terms = local_terms * jnp.exp(local_top - top_score)[:, None]
    posterior = (exp_terms / mass_total[:, None]).astype(jnp.bfloat16).reshape(-1, orient_local)
    weighted = lax.dot_general(
        posterior, shifted, (((0,), (0,)), ((), ())), preferred_element_type=jnp.float32
    )
    post_mass = jnp.sum(posterior.astype(jnp.float32), axis=0)
    own_rows = orient_local // group_count
    own_slices, own_mass = (
        lax.psum_scatter(
            weighted.astype(jnp.bfloat16), ("img", "brick"), scatter_dimension=0, tiled=True
        ).astype(jnp.float32),
        lax.psum_scatter(
            post_mass.astype(jnp.bfloat16), ("img", "brick"), scatter_dimension=0, tiled=True
        ).astype(jnp.float32),
    )
    seg_count = K // SEG
    seg_rows = own_rows * seg_count
    capacity = 2 * ((seg_rows + brick_count - 1) // brick_count)
    brick_table = seg_map[:, 0].reshape(brick_count, seg_rows)
    own_dest = lax.dynamic_index_in_dim(brick_table, flat_index, 0, keepdims=False)
    brick_ids = jnp.arange(brick_count, dtype=jnp.int32)
    brick_hits = (own_dest[:, None] == brick_ids[None, :]).astype(jnp.int32)
    slot_rank = jnp.sum((jnp.cumsum(brick_hits, axis=0) - 1) * brick_hits, axis=1)
    target = own_dest * capacity + slot_rank
    select = (
        jnp.arange(brick_count * capacity, dtype=jnp.int32)[:, None] == target[None, :]
    ).astype(jnp.float32)
    select = select.reshape(brick_count * capacity, own_rows, seg_count)
    pieces = own_slices.reshape(own_rows, 2, seg_count, SEG)
    outgoing = jnp.einsum("qtj,tpjs->qps", select, pieces, precision=lax.Precision.HIGHEST)
    outgoing = outgoing.reshape(brick_count, capacity, 2, SEG)
    outgoing_mass = jnp.einsum(
        "qtj,t->q", select, own_mass, precision=lax.Precision.HIGHEST
    ).reshape(brick_count, capacity)
    arrived, arrived_mass = (
        lax.all_to_all(
            outgoing.astype(jnp.bfloat16),
            ("orient", "img", "brick"),
            split_axis=0,
            concat_axis=0,
            tiled=True,
        ).astype(outgoing.dtype),
        lax.all_to_all(
            outgoing_mass.astype(jnp.bfloat16),
            ("orient", "img", "brick"),
            split_axis=0,
            concat_axis=0,
            tiled=True,
        ).astype(outgoing_mass.dtype),
    )
    arrivals = brick_table == flat_index
    arrival_slot = jnp.cumsum(arrivals.astype(jnp.int32), axis=1) - 1
    slot_place = jnp.where(arrivals, arrival_slot, -1)
    slot_pick = (
        slot_place[:, :, None] == jnp.arange(capacity, dtype=jnp.int32)[None, None, :]
    ).astype(jnp.float32)
    segment_of = jnp.arange(seg_rows, dtype=jnp.int32) % seg_count
    segment_pick = (segment_of[:, None] == jnp.arange(seg_count, dtype=jnp.int32)[None, :]).astype(
        jnp.float32
    )
    routing = jnp.einsum("src,rj->scj", slot_pick, segment_pick, precision=lax.Precision.HIGHEST)
    seg_total = jnp.einsum("scj,scpv->jpv", routing, arrived, precision=lax.Precision.HIGHEST)
    seg_mass = jnp.einsum("scj,sc->j", routing, arrived_mass, precision=lax.Precision.HIGHEST)
    weights = interp[0].astype(jnp.float32) * interp_scale
    brick_values = jnp.einsum("jps,jsv->pv", seg_total, weights, precision=lax.Precision.HIGHEST)
    coverage = jnp.sum(weights, axis=1)
    brick_weight = jnp.einsum("j,jv->v", seg_mass, coverage, precision=lax.Precision.HIGHEST)
    return (brick_values[None], brick_weight[None])


def solution(mesh):
    placed = (
        P(("groups", "orient", "img", "brick"), None),
        P("groups", None),
        P(("groups", "orient"), None),
        P(),
        P(("orient", "img", "brick"), None, None, None),
    )
    return jax.shard_map(
        per_device,
        mesh=mesh,
        in_specs=placed,
        out_specs=(
            P(("groups", "orient", "img", "brick"), None, None),
            P(("groups", "orient", "img", "brick"), None),
        ),
        check_vma=False,
    )
```

profile of v0, /device:TPU:0, one launch (start us, length us, event | category | flops | bytes accessed | tf_op | source)
XLA Modules:
  0.0 226.7 jit_solution(8136047674621850956)
XLA Ops:
  7.2 0.0 all-gather.6.cloned.1.call-start
  7.2 0.7 all-gather.6.cloned.1.call-update
  7.9 0.0 reduce-scatter.2.cloned.1.call-start
  8.0 0.8 reshape.244
  8.8 0.1 reshape.245
  8.8 0.1 broadcast_add_fusion.1
  8.9 0.1 add.200
  9.0 0.1 broadcast_add_fusion
  9.1 0.1 add.205
  9.2 2.1 multiply_reduce_fusion
  11.3 28.9 %all-gather.6.cloned.1.call-done = bf16[128,4096]{1,0:T(8,128)(2,1)} async-done(((bf16[32,4096]{1,0:T(8,128)(2,1)}), bf16[128,4096]{1,0:T(8,128)(2,1)}) %all-gather.6.cloned.1.call-update) | async-done | bytes 1048592 | tf_op jit(solution)/shard_map/all_gather | solution.py:71
  40.2 1.4 slice_convert_fusion.1
  41.7 72.2 %fusion.6 = (bf16[2048,2048]{1,0:T(8,128)(2,1)S(1)}, bf16[2048,2048]{1,0:T(8,128)(2,1)S(1)}) fusion(f32[128,2048]{1,0:T(8,128)S(1)} %get-tuple-element.154, s32[2048]{0:T(1024)S(1)} %get-tuple-element.161, s32[2048]{0:T(1024)S(1)} %add.205, s32[2048]{0:T(1024)S(1)} %get-tuple-element.162, s32[2048]{0:T(1024)S(1)} %add.200, f32[128,2048]{1,0:T(8,128)S(1)} %get-tuple-element.153), kind=kLoop, calls=%fused_computation.17 | loop fusion | flops 100663296 | bytes 18907136 | tf_op jit(solution)/shard_map/convert.2
  113.9 0.0 copy-start
  113.9 0.0 copy-start.1
  113.9 8.9 %fusion.60 = (f32[2048]{0:T(1024)S(1)}, f32[2048,256]{0,1:T(8,128)}) fusion(f32[256]{0:T(256)S(1)} %broadcast_multiply_fusion, bf16[256,4096]{1,0:T(8,128)(2,1)} %param.9, bf16[2048,2048]{1,0:T(8,128)(2,1)S(1)} %get-tuple-element.152, bf16[2048,2048]{1,0:T(8,128)(2,1)S(1)} %get-tuple-element.151), kind=kOutput, calls=%fused_computation.115 | convolution fusion | flops 4330092544 | bytes 20980736 | tf_op jit(solution)/shard_map/dot_general | solution.py:73
  122.9 0.1 reduce_max.14
  123.0 0.1 reduce_max.18
  123.1 0.1 sub.96
  123.1 0.1 sub.97
  123.3 1.9 fusion.25
  125.2 0.1 reduce_sum.70
  125.2 0.1 reduce_sum.71
  125.4 9.4 %all-gather.3 = f32[4,1,128]{2,1,0:T(1,128)S(1)} all-gather(f32[1,1,128]{2,1,0:T(1,128)S(1)} %bitcast.147), channel_id=3, replica_groups=mesh['groups'=2,'orient'=4,'img'=2,'brick'=2] {'orient'}, dimensions={0}, use_global_device_ids=true | all-gather | bytes 2560 | tf_op jit(solution)/shard_map/all_gather | solution.py:16
  134.8 7.6 %all-gather.2 = f32[4,1,128]{2,1,0:T(1,128)S(1)} all-gather(f32[1,1,128]{2,1,0:T(1,128)S(1)} %bitcast.146), channel_id=2, replica_groups=mesh['groups'=2,'orient'=4,'img'=2,'brick'=2] {'orient'}, dimensions={0}, use_global_device_ids=true | all-gather | bytes 2560 | tf_op jit(solution)/shard_map/all_gather | solution.py:16
  142.4 0.1 while.17
  142.5 0.1 mul.173
  142.6 0.1 mul.174
  142.7 0.1 div.33
  142.7 0.1 div.34
  142.8 2.2 fusion.59
  145.1 0.0 copy-start.4
  145.1 10.1 %fusion.13 = bf16[256,4096]{1,0:T(8,128)(2,1)} fusion(bf16[2048,256]{0,1:T(8,128)(2,1)S(1)} %get-tuple-element.150, bf16[2048,2048]{1,0:T(8,128)(2,1)} %copy-done.1, bf16[2048,2048]{1,0:T(8,128)(2,1)} %copy-done), kind=kOutput, calls=%fused_computation.25 | convolution fusion | flops 4329570304 | bytes 19922944 | tf_op jit(solution)/shard_map/dot_general | solution.py:84
  155.2 0.0 reduce-scatter.2.cloned.1.call-update
  155.3 0.5 broadcast.343
  155.8 0.0 copy-done.3
  155.8 0.8 reduce.21
  156.6 1.2 reduce-window.16
  157.8 0.2 slice_reduce_fusion
  158.0 0.1 fusion.37
  158.2 0.1 eq.136
  158.3 0.7 convert_reduce_fusion
  158.9 0.2 copy.39
  159.2 0.0 copy-done.4
  159.2 0.6 dynamic-slice
  160.4 5.9 %all-reduce = bf16[256]{0:T(256)(128)(2,1)S(1)} all-reduce(bf16[256]{0:T(256)(128)(2,1)S(1)} %get-tuple-element.149), channel_id=5, replica_groups=mesh['groups'=2,'orient'=4,'img'=2,'brick'=2] {'img','brick'}, use_global_device_ids=true, to_apply=%region_15.16.clone | all-reduce | flops 256 | bytes 1024
  166.3 0.7 fusion.55
  167.0 0.6 copy.32
  167.6 4.5 %all-to-all-start.1 = ((bf16[16,1,64]{2,1,0:T(2,128)(2,1)}), bf16[16,1,64]{2,1,0:T(2,128)(2,1)S(1)}, u32[]{:S(2)}, u32[]{:S(2)}) async-start(bf16[16,1,64]{2,1,0:T(2,128)(2,1)} %copy.32), calls=%async_computation.2 | async-start | bytes 16384 | tf_op jit(solution)/shard_map/all_to_all | solution.py:124
  172.1 14.3 %reduce-scatter.2.cloned.1.call-done = bf16[64,4096]{1,0:T(8,128)(2,1)} async-done(((bf16[256,4096]{1,0:T(8,128)(2,1)}), bf16[64,4096]{1,0:T(8,128)(2,1)}) %reduce-scatter.2.cloned.1.call-update) | async-done | bytes 524304 | tf_op jit(solution)/shard_map/reduce_scatter | solution.py:90
  186.4 1.1 copy.42
  187.6 2.5 %bitcast_convert_fusion = bf16[16,64,2,256]{3,1,2,0:T(8,128)(2,1)} fusion(s32[8,64]{0,1:T(8,128)S(1)} %bitcast.138, s32[16,64]{1,0:T(8,128)S(1)} %multiply_add_fusion, bf16[64,2,8,256]{3,2,1,0:T(8,128)(2,1)S(1)} %bitcast.137), kind=kOutput, calls=%fused_computation.34 | convolution fusion | flops 537919488 | bytes 1579008 | tf_op jit(solution)/shard_map/qtj,tpjs->qps/dot_general | solution.py:111
  190.0 0.0 all-to-all-done.1
  190.0 4.7 %all-to-all-start = ((bf16[16,64,2,256]{3,1,2,0:T(8,128)(2,1)}), bf16[16,64,2,256]{3,1,2,0:T(8,128)(2,1)S(1)}, u32[]{:S(2)}, u32[]{:S(2)}) async-start(bf16[16,64,2,256]{3,1,2,0:T(8,128)(2,1)} %bitcast_convert_fusion), calls=%async_computation.1 | async-start | bytes 2097152 | tf_op jit(solution)/shard_map/all_to_all | solution.py:117
  194.8 1.2 reduce-window.14
  196.0 0.2 slice_reduce_fusion.1
  196.2 0.2 fusion.24
  196.5 0.1 bitcast_select_fusion
  196.5 0.5 fusion.23
  197.1 0.1 convolution_bitcast_fusion.1
  197.2 0.8 fusion.61
  198.0 19.7 %all-to-all-done = bf16[16,64,2,256]{3,1,2,0:T(8,128)(2,1)S(1)} async-done(((bf16[16,64,2,256]{3,1,2,0:T(8,128)(2,1)}), bf16[16,64,2,256]{3,1,2,0:T(8,128)(2,1)S(1)}, u32[]{:S(2)}, u32[]{:S(2)}) %all-to-all-start) | async-done | bytes 1048608 | tf_op jit(solution)/shard_map/all_to_all | solution.py:117
  217.7 0.5 convolution_bitcast_fusion
  218.3 1.6 fusion.28
  (29 shorter events, 0.3 us)
Async XLA Ops:
  7.2 33.1 %all-gather.6.cloned.1.call-start = ((), (), s32[]{:S(2)}) async-start(), calls=%async_computation.3 | async-start | bytes 1310720 | tf_op jit(solution)/shard_map/all_gather | solution.py:71
  7.9 178.5 %reduce-scatter.2.cloned.1.call-start = ((), (), s32[]{:S(2)}) async-start(), calls=%async_computation.4 | async-start | bytes 2621440 | tf_op jit(solution)/shard_map/reduce_scatter | solution.py:90
  113.9 9.0 %copy-start = (bf16[2048,2048]{1,0:T(8,128)(2,1)}, bf16[2048,2048]{1,0:T(8,128)(2,1)S(1)}, u32[]{:S(2)}) copy-start(bf16[2048,2048]{1,0:T(8,128)(2,1)S(1)} %get-tuple-element.151) | copy-start | bytes 25165828
  113.9 9.0 %copy-start.1 = (bf16[2048,2048]{1,0:T(8,128)(2,1)}, bf16[2048,2048]{1,0:T(8,128)(2,1)S(1)}, u32[]{:S(2)}) copy-start(bf16[2048,2048]{1,0:T(8,128)(2,1)S(1)} %get-tuple-element.152) | copy-start | bytes 25165828
  145.0 10.7 %copy-start.3 = (s32[8192,1]{0,1:T(1,128)S(1)}, s32[8192,1]{0,1:T(1,128)}, u32[]{:S(2)}) copy-start(s32[8192,1]{0,1:T(1,128)} %param.10) | copy-start | bytes 98308
  145.1 14.1 %copy-start.4 = (u32[32]{0:T(128)S(1)}, u32[32]{0:T(128)}, u32[]{:S(2)}) copy-start(u32[32]{0:T(128)} %constant.178) | copy-start | bytes 388
  155.2 41.0 %copy-start.2 = (s32[1,8,256,256]{3,2,1,0:T(8,128)S(1)}, s32[1,8,256,256]{3,2,1,0:T(8,128)}, u32[]{:S(2)}) copy-start(s32[1,8,256,256]{3,2,1,0:T(8,128)} %param.11) | copy-start | bytes 6291460
  167.6 22.4 %all-to-all-start.1 = ((bf16[16,1,64]{2,1,0:T(2,128)(2,1)}), bf16[16,1,64]{2,1,0:T(2,128)(2,1)S(1)}, u32[]{:S(2)}, u32[]{:S(2)}) async-start(bf16[16,1,64]{2,1,0:T(2,128)(2,1)} %copy.32), calls=%async_computation.2 | async-start | bytes 16384 | tf_op jit(solution)/shard_map/all_to_all | solution.py:124
  190.0 27.7 %all-to-all-start = ((bf16[16,64,2,256]{3,1,2,0:T(8,128)(2,1)}), bf16[16,64,2,256]{3,1,2,0:T(8,128)(2,1)S(1)}, u32[]{:S(2)}, u32[]{:S(2)}) async-start(bf16[16,64,2,256]{3,1,2,0:T(8,128)(2,1)} %bitcast_convert_fusion), calls=%async_computation.1 | async-start | bytes 2097152 | tf_op jit(solution)/shard_map/all_to_all | solution.py:117
Sparse Core Ops, SparseCore 0:
  9.6 30.6 all-gather.5
  155.4 31.0 reduce-scatter.1
where the time goes:
time: 228 us; the launch traced here: 227 us
  other arithmetic  84.7 us (37%)
  waiting for transfers between devices  63.7 us (28%)
  matrix products  25.8 us (11%)
  blocking collectives  22.9 us (10%)
  between operations  15 us (7%)
  starting transfers between devices  9.25 us (4%)
  local copies, waits for them, and re-layouts  5.36 us (2%)
    another operation x5, other arithmetic  74.6 us
    all_gather x1, waiting for transfers between devices, per_device(): lax.all_gather(images, 'orient', axis=0, tiled=True)  28.9 us
    all_to_all x1, waiting for transfers between devices, per_device(): lax.all_to_all(outgoing.astype(jnp.bfloat16), ('orient', 'img', 'brick'),...  19.7 us
    all_gather x2, blocking collectives, combined_all(): everything = jax.tree.map(lambda part: lax.all_gather(part, axis), array)  17 us
    reduce_scatter x1, waiting for transfers between devices, per_device(): lax.psum_scatter(weighted.astype(jnp.bfloat16), ('img', 'brick'), scatter...  14.3 us
    dot_general x1, matrix products, per_device(): lax.dot_general(posterior, shifted, (((0,), (0,)), ((), ())), preferred_e...  10.1 us
    dot_general x1, matrix products, per_device(): lax.dot_general(shifted, slices, (((1,), (1,)), ((), ())), preferred_elem...  8.94 us
    unnamed x1, blocking collectives  5.85 us
  transfers between devices with their start and end apart: 4, of which 3 were waited for; matrix products, arithmetic and copies ran while one was open for 7% of the time, Pallas kernels for 0%

commit v1 on v0

v1 whole, which is shorter than its diff:
```python
import functools
import numpy as np
import jax
import jax.numpy as jnp
from jax import lax
from jax.experimental import pallas as pl
from jax.experimental.pallas import tpu as pltpu
from jax.sharding import PartitionSpec as P

SHIFTS = 16
SEG = 256
LANES = 128
frame_side = 64
MESH = pl.DeviceIdType.MESH
f32 = jnp.float32
bf16 = jnp.bfloat16


def turn(index):
    index = index - frame_side * jnp.floor(index * (1.0 / frame_side) + 0.5)
    x = index * f32(np.pi / frame_side)
    y = x * x
    s = x * (1 + y * (-1 / 6 + y * (1 / 120 + y * (-1 / 5040 + y * (1 / 362880 + y * (-1 / 39916800 + y * (1 / 6227020800.0)))))))
    c = 1 + y * (-1 / 2 + y * (1 / 24 + y * (-1 / 720 + y * (1 / 40320 + y * (-1 / 3628800 + y * (1 / 479001600.0))))))
    return 1 - 2 * s * s, 2 * s * c


def nt(a, b):
    return lax.dot_general(a, b, (((1,), (1,)), ((), ())), preferred_element_type=f32)


def body(cfg, images, offs, slices_hbm, seg_t, interp_hbm, cos_tab, sin_tab, values_out, weight_out,
         img_buf, slices, interp, weights, shifted, terms, half_norm, hits, tops, stats, acc, mass_acc,
         msg, inbox, load_sem, send_r, send_l, recv_l, recv_r, stat_send, stat_recv, msg_send, msg_recv):
    n_or, n_img, n_brick, halves = cfg
    n_grp = n_img * n_brick
    n_dev = n_or * n_grp
    per, width = images.shape
    k_count = width // 2
    pp = per // halves
    rows = pp * SHIFTS
    together = max(1, 16 // pp)
    seg_count = k_count // SEG
    orients = slices.shape[0]
    inv_noise = 100.0 / k_count
    o = lax.axis_index("orient")
    group = lax.axis_index("img") * n_brick + lax.axis_index("brick")
    me = o * n_grp + group

    def place(flat):
        return {"orient": flat // n_grp, "img": (flat // n_brick) % n_img, "brick": flat % n_brick}

    load_slices = pltpu.make_async_copy(slices_hbm, slices, load_sem.at[0])
    load_interp = pltpu.make_async_copy(interp_hbm.at[0], interp, load_sem.at[1])
    load_slices.start()
    load_interp.start()

    barrier = pltpu.get_barrier_semaphore()

    def greet(i, c):
        pl.semaphore_signal(barrier, inc=1, device_id=place((me + i) % n_dev), device_id_type=MESH)
        return c

    lax.fori_loop(1, n_dev, greet, 0)
    pl.semaphore_wait(barrier, n_dev - 1)

    def part_of(ref, k, h):
        return ref.at[k, pl.ds(h * pp, pp), :]

    def to_right(t, h):
        k = jnp.maximum(o - t, 0)
        ref = part_of(img_buf, k, h)
        return pltpu.make_async_remote_copy(ref, ref, send_r.at[t, h], recv_l.at[t + 1, h],
                                            device_id={"orient": jnp.minimum(o + 1, n_or - 1)}, device_id_type=MESH)

    def to_left(t, h):
        k = jnp.minimum(o + t, n_or - 1)
        ref = part_of(img_buf, k, h)
        return pltpu.make_async_remote_copy(ref, ref, send_l.at[t, h], recv_r.at[t + 1, h],
                                            device_id={"orient": jnp.maximum(o - 1, 0)}, device_id_type=MESH)

    def from_left(t, h):
        ref = part_of(img_buf, jnp.maximum(o - t, 0), h)
        return pltpu.make_async_remote_copy(ref, ref, send_r.at[t, h], recv_l.at[t, h],
                                            device_id={"orient": jnp.maximum(o - 1, 0)}, device_id_type=MESH)

    def from_right(t, h):
        ref = part_of(img_buf, jnp.minimum(o + t, n_or - 1), h)
        return pltpu.make_async_remote_copy(ref, ref, send_l.at[t, h], recv_r.at[t, h],
                                            device_id={"orient": jnp.minimum(o + 1, n_or - 1)}, device_id_type=MESH)

    img_buf[o] = images[...]
    for h in range(halves):
        @pl.when(o < n_or - 1)
        def _():
            to_right(0, h).start()

        @pl.when(o > 0)
        def _():
            to_left(0, h).start()

    load_slices.wait()

    def squares(b, total):
        block = slices[:, pl.ds(pl.multiple_of(b * LANES, LANES), LANES)].astype(f32)
        return total + block * block

    norm = lax.fori_loop(0, width // LANES, squares, jnp.zeros((orients, LANES), f32))
    norm = 0.5 * jnp.sum(norm, axis=1, keepdims=True)
    diag = lax.broadcasted_iota(jnp.int32, (orients, orients), 0) == lax.broadcasted_iota(jnp.int32, (orients, orients), 1)
    half_norm[...] = jnp.sum(jnp.where(diag, norm, 0.0), axis=0, keepdims=True)

    seg = seg_t[...]

    def hit_rows(b, c):
        hits[b] = jnp.where(seg == b, 1.0, 0.0).astype(f32)
        return c

    lax.fori_loop(0, n_dev, hit_rows, 0)

    acc[...] = jnp.zeros_like(acc)
    mass_acc[...] = jnp.zeros_like(mass_acc)

    lane = lax.broadcasted_iota(jnp.int32, (pp, LANES), 1)
    freq = (lane % frame_side - frame_side // 2).astype(f32)
    odd = (lane // frame_side).astype(f32)
    same = lax.broadcasted_iota(jnp.int32, (pp, LANES), 0) == lane
    row8 = lax.broadcasted_iota(jnp.int32, (8, LANES), 0)
    per_block = LANES // frame_side

    def score(k, h):
        q = k * halves + h
        base = q * rows
        off = offs[pl.ds(pl.multiple_of((k * n_grp + group) * per + h * pp, 8), pp), :]
        a = (off[:, 0:1] - 2).astype(f32)
        b = (off[:, 1:2] - 2).astype(f32)
        start = turn(a * freq + b * odd)
        step_c, step_s = turn(jnp.broadcast_to(b * per_block, (pp, LANES)))

        def columns(kb, cs):
            ec, es = cs
            at_r = pl.ds(pl.multiple_of(kb * LANES, LANES), LANES)
            at_i = pl.ds(pl.multiple_of(k_count + kb * LANES, LANES), LANES)
            xr = img_buf[k, pl.ds(h * pp, pp), at_r].astype(f32)
            xi = img_buf[k, pl.ds(h * pp, pp), at_i].astype(f32)
            yr = xr * ec + xi * es
            yi = xi * ec - xr * es
            for s in range(0, SHIFTS, together):
                zr, zi = [], []
                for e in range(s, s + together):
                    c = cos_tab[e:e + 1, at_r]
                    d = sin_tab[e:e + 1, at_r]
                    zr.append(yr * c + yi * d)
                    zi.append(yi * c - yr * d)
                at = pl.ds(pl.multiple_of(base + s * pp, together * pp), together * pp)
                shifted[at, at_r] = jnp.concatenate(zr, axis=0).astype(bf16)
                shifted[at, at_i] = jnp.concatenate(zi, axis=0).astype(bf16)
            return ec * step_c - es * step_s, es * step_c + ec * step_s

        lax.fori_loop(0, k_count // LANES, columns, start)
        at = pl.ds(pl.multiple_of(base, rows), rows)
        got = inv_noise * (nt(shifted[at, :], slices[...]) - half_norm[...])
        got = got.reshape(SHIFTS, pp, orients)
        top = jnp.max(jnp.max(got, axis=0), axis=1, keepdims=True)
        term = jnp.exp(got - top[None])
        mass = jnp.sum(jnp.sum(term, axis=0), axis=1, keepdims=True)
        terms[at, :] = term.reshape(rows, orients)
        tops[q] = jnp.broadcast_to(top, (pp, LANES))
        top_row = jnp.sum(jnp.where(same, top, 0.0), axis=0, keepdims=True)
        mass_row = jnp.sum(jnp.where(same, mass, 0.0), axis=0, keepdims=True)
        stats[q, 0] = jnp.where(row8 == 0, top_row, mass_row)
        for i in range(1, n_or):
            stat_copy(q, i).start()

    def stat_copy(q, i):
        return pltpu.make_async_remote_copy(stats.at[q, 0], stats.at[q, i], stat_send.at[q, i], stat_recv.at[q, i],
                                            device_id={"orient": (o + i) % n_or}, device_id_type=MESH)

    def distance(step, c):
        t, h = step // halves, step % halves
        has_left = (t > 0) & (o - t >= 0)
        has_right = (t > 0) & (o + t < n_or)

        @pl.when(has_left)
        def _():
            from_left(t, h).wait_recv()

        @pl.when(has_left & (o < n_or - 1))
        def _():
            to_right(t, h).start()

        @pl.when(has_right)
        def _():
            from_right(t, h).wait_recv()

        @pl.when(has_right & (o > 0))
        def _():
            to_left(t, h).start()

        def side(d, c):
            k = o + t * (2 * d - 1)
            live = (k >= 0) & (k < n_or) & ((t > 0) | (d == 0))

            @pl.when(live)
            def _():
                score(k, h)
            return c

        return lax.fori_loop(0, 2, side, c)

    lax.fori_loop(0, n_or * halves, distance, 0)

    load_interp.wait()

    def split(j, c):
        w = interp[j]
        weights[j, :, 0:SEG] = (w >> 4).astype(f32).astype(bf16)
        weights[j, :, SEG:2 * SEG] = (w & 15).astype(f32).astype(bf16)
        return c

    lax.fori_loop(0, seg_count, split, 0)

    hit = hits[...].reshape(n_dev * seg_count, orients).astype(bf16)
    seg_row = lax.broadcasted_iota(jnp.int32, (n_dev * seg_count, SEG), 0) % seg_count

    def collect(step, c):
        m, h = step // halves, step % halves
        if n_or % 2 == 0:
            k = n_or // 2 + (m % 2) * (m // 2) - (1 - m % 2) * (m // 2 + 1)
        else:
            k = m
        q = k * halves + h

        def arrive(i, c):
            stat_copy(q, i).wait_recv()
            return c

        lax.fori_loop(1, n_or, arrive, 0)
        every = [stats[q, i] for i in range(n_or)]
        top = functools.reduce(jnp.maximum, [e[0:1] for e in every])
        mass = functools.reduce(jnp.add, [e[1:2] * jnp.exp(e[0:1] - top) for e in every])
        top = jnp.sum(jnp.where(same, top, 0.0), axis=1, keepdims=True)
        mass = jnp.sum(jnp.where(same, mass, 0.0), axis=1, keepdims=True)
        factor = jnp.exp(tops[q][:, 0:1] - top) / mass
        at = pl.ds(pl.multiple_of(q * rows, rows), rows)
        post = terms[at, :].reshape(SHIFTS, pp, orients) * factor[None]
        post = post.reshape(rows, orients).astype(bf16)
        share = nt(hit, post)
        mass_acc[...] += jnp.broadcast_to(jnp.sum(share, axis=1, keepdims=True), mass_acc.shape)
        share = share.astype(bf16)
        for p in range(2):
            total = acc[p]
            for j in range(seg_count):
                c0 = p * k_count + j * SEG
                got = jnp.dot(share, shifted[at, c0:c0 + SEG], preferred_element_type=f32)
                total = jnp.where(seg_row == j, total + got, total)
            acc[p] = total
        return c

    lax.fori_loop(0, n_or * halves, collect, 0)

    def pack(b, c):
        at = pl.ds(pl.multiple_of(b * seg_count, seg_count), seg_count)
        msg[b, :, 0:SEG] = jnp.concatenate([acc[0, at, :], acc[1, at, :]], axis=0).astype(bf16)
        m = mass_acc[at, :]
        hi = m.astype(bf16).astype(f32)
        msg[b, :, SEG:SEG + LANES] = jnp.concatenate([hi, m - hi], axis=0).astype(bf16)
        return c

    lax.fori_loop(0, n_dev, pack, 0)

    def msg_copy(i):
        to = (me + i) % n_dev
        return pltpu.make_async_remote_copy(msg.at[to], inbox.at[i], msg_send.at[i], msg_recv.at[i],
                                            device_id=place(to), device_id_type=MESH)

    def post_msg(i, c):
        msg_copy(i).start()
        return c

    lax.fori_loop(1, n_dev, post_msg, 0)

    def take(i, total):
        msg_copy(i).wait_recv()
        return total + inbox[i].astype(f32)

    total = lax.fori_loop(1, n_dev, take, msg[me].astype(f32))
    mass = total[0:seg_count, SEG:] + total[seg_count:, SEG:]
    left = jnp.concatenate([total[:, 0:SEG], jnp.concatenate([mass, mass], axis=1)], axis=0)
    n_rows = 3 * seg_count
    hi = left.astype(bf16).astype(f32)
    both = jnp.concatenate([hi, left - hi], axis=0).astype(bf16)
    place_row = lax.broadcasted_iota(jnp.int32, (n_rows, SEG), 0) % seg_count
    result = jnp.zeros((n_rows, SEG), f32)
    for j in range(seg_count):
        got = jnp.dot(both, weights[j], preferred_element_type=f32)
        got = got[0:n_rows] + got[n_rows:]
        got = got[:, 0:SEG] * (16.0 / 256.0) + got[:, SEG:] * (1.0 / 256.0)
        result = jnp.where(place_row == j, got, result)
    result = jnp.sum(result.reshape(3, seg_count, SEG), axis=1)
    values_out[...] = result[0:2]
    weight_out[...] = result[2:3]

    def settle(step, c):
        t, h = step // halves, step % halves

        @pl.when((o < n_or - 1) & (o - t >= 0))
        def _():
            to_right(t, h).wait_send()

        @pl.when((o > 0) & (o + t < n_or))
        def _():
            to_left(t, h).wait_send()
        return c

    lax.fori_loop(0, (n_or - 1) * halves, settle, 0)

    def settle_stats(q, c):
        for i in range(1, n_or):
            stat_copy(q, i).wait_send()
        return c

    lax.fori_loop(0, n_or * halves, settle_stats, 0)

    def settle_msgs(i, c):
        msg_copy(i).wait_send()
        return c

    lax.fori_loop(1, n_dev, settle_msgs, 0)


def per_device(images, offsets, slices, seg_map, interp):
    n_or = lax.axis_size("orient")
    n_img = lax.axis_size("img")
    n_brick = lax.axis_size("brick")
    n_dev = n_or * n_img * n_brick
    per, width = images.shape
    k_count = width // 2
    seg_count = k_count // SEG
    orients = slices.shape[0]
    halves = 2 if per % 32 == 0 else 1
    pp = per // halves
    rows = pp * SHIFTS
    pieces = n_or * halves
    coef = np.arange(k_count)
    shift = np.arange(SHIFTS)
    index = ((shift % 4)[:, None] * (coef % frame_side - frame_side // 2)[None, :]
             + (shift // 4)[:, None] * (coef // frame_side)[None, :]) % frame_side
    angle = 2 * np.pi * index / frame_side
    cos_tab = jnp.asarray(np.cos(angle), f32)
    sin_tab = jnp.asarray(np.sin(angle), f32)
    own_seg = lax.dynamic_index_in_dim(
        seg_map.reshape(n_or, orients, seg_count), lax.axis_index("orient"), 0, keepdims=False).T
    vmem = pl.BlockSpec(memory_space=pltpu.VMEM)
    hbm = pl.BlockSpec(memory_space=pl.ANY)
    dma = pltpu.SemaphoreType.DMA
    values, weight = pl.pallas_call(
        functools.partial(body, (n_or, n_img, n_brick, halves)),
        out_shape=(jax.ShapeDtypeStruct((2, SEG), f32), jax.ShapeDtypeStruct((1, SEG), f32)),
        in_specs=[vmem, vmem, hbm, vmem, hbm, vmem, vmem],
        out_specs=(vmem, vmem),
        scratch_shapes=[
            pltpu.VMEM((n_or, per, width), bf16),
            pltpu.VMEM((orients, width), bf16),
            pltpu.VMEM((seg_count, SEG, SEG), jnp.int32),
            pltpu.VMEM((seg_count, SEG, 2 * SEG), bf16),
            pltpu.VMEM((pieces * rows, width), bf16),
            pltpu.VMEM((pieces * rows, orients), f32),
            pltpu.VMEM((1, orients), f32),
            pltpu.VMEM((n_dev, seg_count, orients), f32),
            pltpu.VMEM((pieces, pp, LANES), f32),
            pltpu.VMEM((pieces, n_or, 8, LANES), f32),
            pltpu.VMEM((2, n_dev * seg_count, SEG), f32),
            pltpu.VMEM((n_dev * seg_count, LANES), f32),
            pltpu.VMEM((n_dev, 2 * seg_count, SEG + LANES), bf16),
            pltpu.VMEM((n_dev, 2 * seg_count, SEG + LANES), bf16),
            dma((2,)),
            dma((n_or, halves)),
            dma((n_or, halves)),
            dma((n_or + 1, halves)),
            dma((n_or + 1, halves)),
            dma((pieces, n_or)),
            dma((pieces, n_or)),
            dma((n_dev,)),
            dma((n_dev,)),
        ],
        compiler_params=pltpu.CompilerParams(
            collective_id=0, has_side_effects=True, vmem_limit_bytes=56 * 1024 * 1024),
        name="score_and_insert",
    )(images, offsets, slices, own_seg, interp, cos_tab, sin_tab)
    return values[None], weight


def solution(mesh):
    placed = (
        P(("groups", "orient", "img", "brick"), None),
        P("groups", None),
        P(("groups", "orient"), None),
        P(),
        P(("orient", "img", "brick"), None, None, None),
    )
    return jax.shard_map(
        per_device,
        mesh=mesh,
        in_specs=placed,
        out_specs=(
            P(("groups", "orient", "img", "brick"), None, None),
            P(("groups", "orient", "img", "brick"), None),
        ),
        check_vma=False,
    )
```

time: 228 us -> 52.4 us (0.23)
  other arithmetic: 84.7 us -> 1.48 us
  waiting for transfers between devices: 63.7 us -> 0 us
  Pallas kernels: 0 us -> 44.5 us
  matrix products: 25.8 us -> 0 us
  blocking collectives: 22.9 us -> 0 us
  between operations: 15 us -> 0.66 us
  starting transfers between devices: 9.25 us -> 0 us
    another operation x5 -> x0, other arithmetic: 74.6 us -> none
    pallas_call x0 -> x1, Pallas kernels: none -> 44.5 us  [per_device(): pl.pallas_call(functools.partial(body, (n_or, n_img, n_brick, halves)), o...]
    all_gather x1 -> x0, waiting for transfers between devices: 28.9 us -> none  [per_device(): lax.all_gather(images, 'orient', axis=0, tiled=True)]
    dot_general x9 -> x0, matrix products: 25.8 us -> none  [the longest x1 10.1 us: per_device(): lax.dot_general(posterior, shifted, (((0,), (0,)), ((), ())), preferred_e...]
    all_to_all x2 -> x0, waiting for transfers between devices: 19.7 us -> none  [the longest x1 19.7 us: per_device(): lax.all_to_all(outgoing.astype(jnp.bfloat16), ('orient', 'img', 'brick'),...]
    all_gather x2 -> x0, blocking collectives: 17 us -> none  [combined_all(): everything = jax.tree.map(lambda part: lax.all_gather(part, axis), array)]
    reduce_scatter x1 -> x0, waiting for transfers between devices: 14.3 us -> none  [per_device(): lax.psum_scatter(weighted.astype(jnp.bfloat16), ('img', 'brick'), scatter...]
    all_to_all x2 -> x0, starting transfers between devices: 9.17 us -> none  [the longest x1 4.71 us: per_device(): lax.all_to_all(outgoing.astype(jnp.bfloat16), ('orient', 'img', 'brick'),...]
  transfers between devices with their start and end apart: 4 -> 0, of which waited for: 3 -> 0; matrix products, arithmetic and copies ran while one was open for 7% -> 0% of each run, Pallas kernels for 0% -> 0%
where the time goes in v1:
time: 52.4 us; the launch traced here: 52.1 us
  Pallas kernels  44.5 us (85%)
  local copies, waits for them, and re-layouts  5.49 us (10%)
  other arithmetic  1.48 us (3%)
  between operations  0.66 us (1%)
    pallas_call x1, Pallas kernels, per_device(): pl.pallas_call(functools.partial(body, (n_or, n_img, n_brick, halves)), o...  44.5 us
    unnamed x4, local copies, waits for them, and re-layouts  4.52 us
    unnamed x1, other arithmetic  1.48 us

profile of v1, /device:TPU:0, one launch (start us, length us, event | category | flops | bytes accessed | tf_op | source)
XLA Modules:
  0.0 52.1 jit_solution(18001567038060583541)
XLA Ops:
  0.6 0.5 broadcast.3
  1.1 1.5 %reduce.3 = s32[8192]{0:T(1024)S(1)} reduce(s32[8192,1]{0,1:T(1,128)} %param.10, s32[]{:T(128)} %broadcast.3), dimensions={1}, to_apply=%param.10.reduce_sub_computation.3 | reduce | bytes 65540 | tf_op args[3]
  2.6 0.3 reshape.7
  3.0 0.7 %copy.11 = s32[1,256,8]{1,2,0:T(8,128)} copy(s32[1,256,8]{2,1,0:T(8,128)S(1)} %constant_dynamic-slice_fusion) | data formatting | bytes 16384 | tf_op jit(solution)/shard_map/jit(dynamic_index_in_dim)/dynamic_slice | solution.py:352
  3.6 1.5 %copy.12.offs = s32[512,2]{1,0:T(8,128)} copy(s32[512,2]{0,1:T(2,128)} %param.8) | data formatting | bytes 8192 | tf_op args[1]
  5.1 44.5 %score_and_insert.1 = (f32[2,256]{1,0:T(2,128)}, f32[1,256]{1,0:T(1,128)}) custom-call(bf16[32,4096]{1,0:T(8,128)(2,1)} %images.1, s32[512,2]{1,0:T(8,128)} %copy.12.offs, bf16[256,4096]{1,0:T(8,128)(2,1)} %slices_hbm.1, s32[8,256]{1,0:T(8,128)} %bitcast.5, s32[1,8,256,256]{3,2,1,0:T(8,128)} %interp_hbm.1, f32[16,2048]{1,0:T(8,128)} %constant.15.clone.cos_tab, ...), custom_call_target="tpu_custom_call" | custom-call | tf_op jit(solution)/shard_map/score_and_insert/pallas_call | solution.py:357
  49.6 1.2 %copy.15 = f32[1,2,256]{2,1,0:T(2,128)} copy(f32[1,2,256]{2,1,0:T(2,128)} %bitcast.6) | data formatting | bytes 4096
  50.9 1.2 %copy.16 = f32[1,256]{1,0:T(1,128)} copy(f32[1,256]{1,0:T(1,128)} %get-tuple-element.9) | data formatting | bytes 2048
  (1 shorter events, 0.0 us)

commit v2 on v1

--- a/solution.py
+++ b/solution.py
@@ -29,8 +29,8 @@
     return lax.dot_general(a, b, (((1,), (1,)), ((), ())), preferred_element_type=f32)
 
 
-def body(cfg, images, offs, slices_hbm, seg_t, interp_hbm, cos_tab, sin_tab, values_out, weight_out,
-         img_buf, slices, interp, weights, shifted, terms, half_norm, hits, tops, stats, acc, mass_acc,
+def body(cfg, images, offs, slices_hbm, seg_map, interp_hbm, cos_tab, sin_tab, result_out,
+         img_buf, slices, interp, weights, shifted, terms, half_norm, hits, tops, stats, shares, off_a, off_b, acc, mass_acc,
          msg, inbox, load_sem, send_r, send_l, recv_l, recv_r, stat_send, stat_recv, msg_send, msg_recv):
     n_or, n_img, n_brick, halves = cfg
     n_grp = n_img * n_brick
@@ -110,7 +110,27 @@
     diag = lax.broadcasted_iota(jnp.int32, (orients, orients), 0) == lax.broadcasted_iota(jnp.int32, (orients, orients), 1)
     half_norm[...] = jnp.sum(jnp.where(diag, norm, 0.0), axis=0, keepdims=True)
 
-    seg = seg_t[...]
+    span = SEG // seg_count
+    seg_lane = lax.broadcasted_iota(jnp.int32, (seg_count, SEG), 1) % seg_count
+    own_j = seg_lane == lax.broadcasted_iota(jnp.int32, (seg_count, SEG), 0)
+    src = lax.broadcasted_iota(jnp.int32, (SEG, orients), 0) // seg_count
+    dst = lax.broadcasted_iota(jnp.int32, (SEG, orients), 1)
+
+    def regroup(t, total):
+        at = pl.ds(pl.multiple_of((o * orients + t * span) * seg_count, SEG), SEG)
+        ids = jnp.where(own_j, seg_map[:, at].astype(f32), 0.0).astype(bf16)
+        to = jnp.where(src + t * span == dst, 1.0, 0.0).astype(bf16)
+        return total + jnp.dot(ids, to, preferred_element_type=f32)
+
+    seg = lax.fori_loop(0, orients // span, regroup, jnp.zeros((seg_count, orients), f32)).astype(jnp.int32)
+
+    image_rows = n_or * per
+    picked = lax.broadcasted_iota(jnp.int32, (image_rows, image_rows * n_grp), 0)
+    picked = ((picked // per) * n_grp + group) * per + picked % per
+    picked = picked == lax.broadcasted_iota(jnp.int32, (image_rows, image_rows * n_grp), 1)
+    off = (offs[...] - 2).astype(f32)
+    for ref, row in ((off_a, off[0:1]), (off_b, off[1:2])):
+        ref[...] = jnp.broadcast_to(jnp.sum(jnp.where(picked, row, 0.0), axis=1, keepdims=True), (image_rows, LANES))
 
     def hit_rows(b, c):
         hits[b] = jnp.where(seg == b, 1.0, 0.0).astype(f32)
@@ -118,7 +138,6 @@
 
     lax.fori_loop(0, n_dev, hit_rows, 0)
 
-    acc[...] = jnp.zeros_like(acc)
     mass_acc[...] = jnp.zeros_like(mass_acc)
 
     lane = lax.broadcasted_iota(jnp.int32, (pp, LANES), 1)
@@ -131,11 +150,11 @@
     def score(k, h):
         q = k * halves + h
         base = q * rows
-        off = offs[pl.ds(pl.multiple_of((k * n_grp + group) * per + h * pp, 8), pp), :]
-        a = (off[:, 0:1] - 2).astype(f32)
-        b = (off[:, 1:2] - 2).astype(f32)
+        at_image = pl.ds(pl.multiple_of(k * per + h * pp, 8), pp)
+        a = off_a[at_image, :]
+        b = off_b[at_image, :]
         start = turn(a * freq + b * odd)
-        step_c, step_s = turn(jnp.broadcast_to(b * per_block, (pp, LANES)))
+        step_c, step_s = turn(b * per_block)
 
         def columns(kb, cs):
             ec, es = cs
@@ -208,27 +227,11 @@
 
         return lax.fori_loop(0, 2, side, c)
 
-    lax.fori_loop(0, n_or * halves, distance, 0)
-
-    load_interp.wait()
-
-    def split(j, c):
-        w = interp[j]
-        weights[j, :, 0:SEG] = (w >> 4).astype(f32).astype(bf16)
-        weights[j, :, SEG:2 * SEG] = (w & 15).astype(f32).astype(bf16)
-        return c
-
-    lax.fori_loop(0, seg_count, split, 0)
-
-    hit = hits[...].reshape(n_dev * seg_count, orients).astype(bf16)
+    hit_all = hits.reshape(n_dev * seg_count, orients)
     seg_row = lax.broadcasted_iota(jnp.int32, (n_dev * seg_count, SEG), 0) % seg_count
 
     def collect(step, c):
-        m, h = step // halves, step % halves
-        if n_or % 2 == 0:
-            k = n_or // 2 + (m % 2) * (m // 2) - (1 - m % 2) * (m // 2 + 1)
-        else:
-            k = m
+        k, h = c + step // halves, step % halves
         q = k * halves + h
 
         def arrive(i, c):
@@ -245,19 +248,48 @@
         at = pl.ds(pl.multiple_of(q * rows, rows), rows)
         post = terms[at, :].reshape(SHIFTS, pp, orients) * factor[None]
         post = post.reshape(rows, orients).astype(bf16)
-        share = nt(hit, post)
+        share = nt(hit_all[...].astype(bf16), post)
         mass_acc[...] += jnp.broadcast_to(jnp.sum(share, axis=1, keepdims=True), mass_acc.shape)
-        share = share.astype(bf16)
+        shares[:, at] = share.astype(bf16)
+        return c
+
+    def gather_in(first, last, fresh):
+        lax.fori_loop(0, (last - first) * halves, collect, first)
+        lo, hi = first * halves * rows, last * halves * rows
         for p in range(2):
-            total = acc[p]
+            total = None if fresh else acc[p]
             for j in range(seg_count):
                 c0 = p * k_count + j * SEG
-                got = jnp.dot(share, shifted[at, c0:c0 + SEG], preferred_element_type=f32)
-                total = jnp.where(seg_row == j, total + got, total)
+                got = jnp.dot(shares[:, lo:hi], shifted[lo:hi, c0:c0 + SEG], preferred_element_type=f32)
+                if fresh:
+                    total = got if total is None else jnp.where(seg_row == j, got, total)
+                else:
+                    total = jnp.where(seg_row == j, total + got, total)
             acc[p] = total
-        return c
-
-    lax.fori_loop(0, n_or * halves, collect, 0)
+
+    quarter = n_or // 4
+    steps = n_or * halves
+    early = (n_or - 1) * halves if quarter else steps
+    lax.fori_loop(0, early, distance, 0)
+    if quarter:
+        gather_in(quarter, n_or - quarter, True)
+        lax.fori_loop(early, steps, distance, 0)
+
+    load_interp.wait()
+
+    def split(j, c):
+        w = interp[j]
+        weights[j, :, 0:SEG] = (w >> 4).astype(f32).astype(bf16)
+        weights[j, :, SEG:2 * SEG] = (w & 15).astype(f32).astype(bf16)
+        return c
+
+    lax.fori_loop(0, seg_count, split, 0)
+
+    if quarter:
+        gather_in(0, quarter, False)
+        gather_in(n_or - quarter, n_or, False)
+    else:
+        gather_in(0, n_or, True)
 
     def pack(b, c):
         at = pl.ds(pl.multiple_of(b * seg_count, seg_count), seg_count)
@@ -298,8 +330,7 @@
         got = got[:, 0:SEG] * (16.0 / 256.0) + got[:, SEG:] * (1.0 / 256.0)
         result = jnp.where(place_row == j, got, result)
     result = jnp.sum(result.reshape(3, seg_count, SEG), axis=1)
-    values_out[...] = result[0:2]
-    weight_out[...] = result[2:3]
+    result_out[...] = result
 
     def settle(step, c):
         t, h = step // halves, step % halves
@@ -327,6 +358,11 @@
         return c
 
     lax.fori_loop(1, n_dev, settle_msgs, 0)
+
+
+def hand_out(result, values_out, weight_out):
+    values_out[0] = result[0:2]
+    weight_out[...] = result[2:3]
 
 
 def per_device(images, offsets, slices, seg_map, interp):
@@ -349,16 +385,14 @@
     angle = 2 * np.pi * index / frame_side
     cos_tab = jnp.asarray(np.cos(angle), f32)
     sin_tab = jnp.asarray(np.sin(angle), f32)
-    own_seg = lax.dynamic_index_in_dim(
-        seg_map.reshape(n_or, orients, seg_count), lax.axis_index("orient"), 0, keepdims=False).T
     vmem = pl.BlockSpec(memory_space=pltpu.VMEM)
     hbm = pl.BlockSpec(memory_space=pl.ANY)
     dma = pltpu.SemaphoreType.DMA
-    values, weight = pl.pallas_call(
+    result = pl.pallas_call(
         functools.partial(body, (n_or, n_img, n_brick, halves)),
-        out_shape=(jax.ShapeDtypeStruct((2, SEG), f32), jax.ShapeDtypeStruct((1, SEG), f32)),
+        out_shape=jax.ShapeDtypeStruct((3, SEG), f32),
         in_specs=[vmem, vmem, hbm, vmem, hbm, vmem, vmem],
-        out_specs=(vmem, vmem),
+        out_specs=vmem,
         scratch_shapes=[
             pltpu.VMEM((n_or, per, width), bf16),
             pltpu.VMEM((orients, width), bf16),
@@ -370,6 +404,9 @@
             pltpu.VMEM((n_dev, seg_count, orients), f32),
             pltpu.VMEM((pieces, pp, LANES), f32),
             pltpu.VMEM((pieces, n_or, 8, LANES), f32),
+            pltpu.VMEM((n_dev * seg_count, pieces * rows), bf16),
+            pltpu.VMEM((n_or * per, LANES), f32),
+            pltpu.VMEM((n_or * per, LANES), f32),
             pltpu.VMEM((2, n_dev * seg_count, SEG), f32),
             pltpu.VMEM((n_dev * seg_count, LANES), f32),
             pltpu.VMEM((n_dev, 2 * seg_count, SEG + LANES), bf16),
@@ -387,8 +424,14 @@
         compiler_params=pltpu.CompilerParams(
             collective_id=0, has_side_effects=True, vmem_limit_bytes=56 * 1024 * 1024),
         name="score_and_insert",
-    )(images, offsets, slices, own_seg, interp, cos_tab, sin_tab)
-    return values[None], weight
+    )(images, offsets.T, slices, seg_map.T, interp, cos_tab, sin_tab)
+    return pl.pallas_call(
+        hand_out,
+        out_shape=(jax.ShapeDtypeStruct((1, 2, SEG), f32), jax.ShapeDtypeStruct((1, SEG), f32)),
+        in_specs=[vmem],
+        out_specs=(vmem, vmem),
+        name="hand_out",
+    )(result)
 
 
 def solution(mesh):

time: 52.4 us -> 48.3 us (0.922)
  local copies, waits for them, and re-layouts: 5.49 us -> 0 us
  Pallas kernels: 44.5 us -> 47.5 us
  other arithmetic: 1.48 us -> 0 us
    unnamed x4 -> x0, local copies, waits for them, and re-layouts: 4.52 us -> none
    pallas_call x1, Pallas kernels: 44.5 us -> 46.3 us  [per_device(): pl.pallas_call(functools.partial(body, (n_or, n_img, n_brick, halves)), o...]
    unnamed x1 -> x0, other arithmetic: 1.48 us -> none
    pallas_call x0 -> x1, Pallas kernels: none -> 1.26 us  [per_device(): pl.pallas_call(hand_out, out_shape=(jax.ShapeDtypeStruct((1, 2, SEG), f32...]
    dynamic_slice x2 -> x0, local copies, waits for them, and re-layouts: 0.68 us -> none  [per_device(): lax.dynamic_index_in_dim(seg_map.reshape(n_or, orients, seg_count), lax.a...]
where the time goes in v2:
time: 48.3 us; the launch traced here: 48.2 us
  Pallas kernels  47.5 us (98%)
  between operations  0.64 us (1%)
    pallas_call x1, Pallas kernels, per_device(): pl.pallas_call(functools.partial(body, (n_or, n_img, n_brick, halves)), o...  46.3 us
    pallas_call x1, Pallas kernels, per_device(): pl.pallas_call(hand_out, out_shape=(jax.ShapeDtypeStruct((1, 2, SEG), f32...  1.26 us

profile of v2, /device:TPU:0, one launch (start us, length us, event | category | flops | bytes accessed | tf_op | source)
XLA Modules:
  0.0 48.2 jit_solution(15925848042413248219)
XLA Ops:
  0.6 46.3 %score_and_insert.1.result = f32[3,256]{1,0:T(4,128)} custom-call(bf16[32,4096]{1,0:T(8,128)(2,1)} %images.1, s32[2,512]{1,0:T(2,128)} %bitcast.3, bf16[256,4096]{1,0:T(8,128)(2,1)} %slices_hbm.1, s32[1,8192]{1,0:T(1,128)} %bitcast.2, s32[1,8,256,256]{3,2,1,0:T(8,128)} %interp_hbm.1, f32[16,2048]{1,0:T(8,128)} %constant.4.clone.cos_tab, ...), custom_call_target="tpu_custom_call" | custom-call | tf_op jit(solution)/shard_map/score_and_insert/pallas_call | solution.py:391
  46.9 1.3 %hand_out.1 = (f32[1,2,256]{2,1,0:T(2,128)}, f32[1,256]{1,0:T(1,128)}) custom-call(f32[3,256]{1,0:T(4,128)} %score_and_insert.1.result), custom_call_target="tpu_custom_call" | custom-call | tf_op jit(solution)/shard_map/hand_out/pallas_call | solution.py:428

commit v3 on v2

--- a/solution.py
+++ b/solution.py
@@ -30,7 +30,7 @@
 
 
 def body(cfg, images, offs, slices_hbm, seg_map, interp_hbm, cos_tab, sin_tab, result_out,
-         img_buf, slices, interp, weights, shifted, terms, half_norm, hits, tops, stats, shares, off_a, off_b, acc, mass_acc,
+         img_buf, slices, interp, weights, shifted, terms, half_norm, hits, tops, stats, shares, off_a, off_b, acc, by_brick, mass_acc,
          msg, inbox, load_sem, send_r, send_l, recv_l, recv_r, stat_send, stat_recv, msg_send, msg_recv):
     n_or, n_img, n_brick, halves = cfg
     n_grp = n_img * n_brick
@@ -62,6 +62,34 @@
         return c
 
     lax.fori_loop(1, n_dev, greet, 0)
+
+    span = SEG // seg_count
+    seg_lane = lax.broadcasted_iota(jnp.int32, (seg_count, SEG), 1) % seg_count
+    own_j = seg_lane == lax.broadcasted_iota(jnp.int32, (seg_count, SEG), 0)
+    src = lax.broadcasted_iota(jnp.int32, (SEG, orients), 0) // seg_count
+    dst = lax.broadcasted_iota(jnp.int32, (SEG, orients), 1)
+
+    def regroup(t, total):
+        at = pl.ds(pl.multiple_of((o * orients + t * span) * seg_count, SEG), SEG)
+        ids = jnp.where(own_j, seg_map[:, at].astype(f32), 0.0).astype(bf16)
+        to = jnp.where(src + t * span == dst, 1.0, 0.0).astype(bf16)
+        return total + jnp.dot(ids, to, preferred_element_type=f32)
+
+    seg = lax.fori_loop(0, orients // span, regroup, jnp.zeros((seg_count, orients), f32)).astype(jnp.int32)
+
+    image_rows = n_or * per
+    picked = lax.broadcasted_iota(jnp.int32, (image_rows, image_rows * n_grp), 0)
+    picked = ((picked // per) * n_grp + group) * per + picked % per
+    picked = picked == lax.broadcasted_iota(jnp.int32, (image_rows, image_rows * n_grp), 1)
+    off = offs[...].astype(f32) - 0.5
+    for ref, row in ((off_a, off[0:1]), (off_b, off[1:2])):
+        ref[...] = jnp.broadcast_to(jnp.sum(jnp.where(picked, row, 0.0), axis=1, keepdims=True), (image_rows, LANES))
+
+    brick = lax.broadcasted_iota(jnp.int32, (n_dev, orients), 0)
+    for j in range(seg_count):
+        hits[j] = jnp.where(seg[j:j + 1] == brick, 1.0, 0.0).astype(bf16)
+
+    img_buf[o] = images[...]
     pl.semaphore_wait(barrier, n_dev - 1)
 
     def part_of(ref, k, h):
@@ -89,7 +117,6 @@
         return pltpu.make_async_remote_copy(ref, ref, send_l.at[t, h], recv_r.at[t, h],
                                             device_id={"orient": jnp.minimum(o + 1, n_or - 1)}, device_id_type=MESH)
 
-    img_buf[o] = images[...]
     for h in range(halves):
         @pl.when(o < n_or - 1)
         def _():
@@ -109,34 +136,6 @@
     norm = 0.5 * jnp.sum(norm, axis=1, keepdims=True)
     diag = lax.broadcasted_iota(jnp.int32, (orients, orients), 0) == lax.broadcasted_iota(jnp.int32, (orients, orients), 1)
     half_norm[...] = jnp.sum(jnp.where(diag, norm, 0.0), axis=0, keepdims=True)
-
-    span = SEG // seg_count
-    seg_lane = lax.broadcasted_iota(jnp.int32, (seg_count, SEG), 1) % seg_count
-    own_j = seg_lane == lax.broadcasted_iota(jnp.int32, (seg_count, SEG), 0)
-    src = lax.broadcasted_iota(jnp.int32, (SEG, orients), 0) // seg_count
-    dst = lax.broadcasted_iota(jnp.int32, (SEG, orients), 1)
-
-    def regroup(t, total):
-        at = pl.ds(pl.multiple_of((o * orients + t * span) * seg_count, SEG), SEG)
-        ids = jnp.where(own_j, seg_map[:, at].astype(f32), 0.0).astype(bf16)
-        to = jnp.where(src + t * span == dst, 1.0, 0.0).astype(bf16)
-        return total + jnp.dot(ids, to, preferred_element_type=f32)
-
-    seg = lax.fori_loop(0, orients // span, regroup, jnp.zeros((seg_count, orients), f32)).astype(jnp.int32)
-
-    image_rows = n_or * per
-    picked = lax.broadcasted_iota(jnp.int32, (image_rows, image_rows * n_grp), 0)
-    picked = ((picked // per) * n_grp + group) * per + picked % per
-    picked = picked == lax.broadcasted_iota(jnp.int32, (image_rows, image_rows * n_grp), 1)
-    off = (offs[...] - 2).astype(f32)
-    for ref, row in ((off_a, off[0:1]), (off_b, off[1:2])):
-        ref[...] = jnp.broadcast_to(jnp.sum(jnp.where(picked, row, 0.0), axis=1, keepdims=True), (image_rows, LANES))
-
-    def hit_rows(b, c):
-        hits[b] = jnp.where(seg == b, 1.0, 0.0).astype(f32)
-        return c
-
-    lax.fori_loop(0, n_dev, hit_rows, 0)
 
     mass_acc[...] = jnp.zeros_like(mass_acc)
 
@@ -164,19 +163,21 @@
             xi = img_buf[k, pl.ds(h * pp, pp), at_i].astype(f32)
             yr = xr * ec + xi * es
             yi = xi * ec - xr * es
-            for s in range(0, SHIFTS, together):
-                zr, zi = [], []
-                for e in range(s, s + together):
-                    c = cos_tab[e:e + 1, at_r]
-                    d = sin_tab[e:e + 1, at_r]
-                    zr.append(yr * c + yi * d)
-                    zi.append(yi * c - yr * d)
-                at = pl.ds(pl.multiple_of(base + s * pp, together * pp), together * pp)
-                shifted[at, at_r] = jnp.concatenate(zr, axis=0).astype(bf16)
-                shifted[at, at_i] = jnp.concatenate(zi, axis=0).astype(bf16)
+            zr, zi = [None] * SHIFTS, [None] * SHIFTS
+            for e in range(SHIFTS // 2):
+                c = cos_tab[e:e + 1, at_r]
+                d = sin_tab[e:e + 1, at_r]
+                rc, rd, ic, id_ = yr * c, yr * d, yi * c, yi * d
+                zr[e], zi[e] = rc + id_, ic - rd
+                zr[SHIFTS - 1 - e], zi[SHIFTS - 1 - e] = rc - id_, ic + rd
+                if (e + 1) % together == 0:
+                    for s in (e + 1 - together, SHIFTS - 1 - e):
+                        at = pl.ds(pl.multiple_of(base + s * pp, together * pp), together * pp)
+                        shifted[at, at_r] = jnp.concatenate(zr[s:s + together], axis=0).astype(bf16)
+                        shifted[at, at_i] = jnp.concatenate(zi[s:s + together], axis=0).astype(bf16)
             return ec * step_c - es * step_s, es * step_c + ec * step_s
 
-        lax.fori_loop(0, k_count // LANES, columns, start)
+        lax.fori_loop(0, k_count // LANES, columns, start, unroll=2)
         at = pl.ds(pl.multiple_of(base, rows), rows)
         got = inv_noise * (nt(shifted[at, :], slices[...]) - half_norm[...])
         got = got.reshape(SHIFTS, pp, orients)
@@ -227,8 +228,6 @@
 
         return lax.fori_loop(0, 2, side, c)
 
-    hit_all = hits.reshape(n_dev * seg_count, orients)
-    seg_row = lax.broadcasted_iota(jnp.int32, (n_dev * seg_count, SEG), 0) % seg_count
 
     def collect(step, c):
         k, h = c + step // halves, step % halves
@@ -248,7 +247,7 @@
         at = pl.ds(pl.multiple_of(q * rows, rows), rows)
         post = terms[at, :].reshape(SHIFTS, pp, orients) * factor[None]
         post = post.reshape(rows, orients).astype(bf16)
-        share = nt(hit_all[...].astype(bf16), post)
+        share = nt(hits[...].reshape(seg_count * n_dev, orients), post)
         mass_acc[...] += jnp.broadcast_to(jnp.sum(share, axis=1, keepdims=True), mass_acc.shape)
         shares[:, at] = share.astype(bf16)
         return c
@@ -257,15 +256,11 @@
         lax.fori_loop(0, (last - first) * halves, collect, first)
         lo, hi = first * halves * rows, last * halves * rows
         for p in range(2):
-            total = None if fresh else acc[p]
             for j in range(seg_count):
                 c0 = p * k_count + j * SEG
-                got = jnp.dot(shares[:, lo:hi], shifted[lo:hi, c0:c0 + SEG], preferred_element_type=f32)
-                if fresh:
-                    total = got if total is None else jnp.where(seg_row == j, got, total)
-                else:
-                    total = jnp.where(seg_row == j, total + got, total)
-            acc[p] = total
+                got = jnp.dot(shares[j * n_dev:(j + 1) * n_dev, lo:hi], shifted[lo:hi, c0:c0 + SEG],
+                              preferred_element_type=f32)
+                acc[p, j] = got if fresh else acc[p, j] + got
 
     quarter = n_or // 4
     steps = n_or * halves
@@ -291,10 +286,20 @@
     else:
         gather_in(0, n_or, True)
 
+    for j in range(seg_count):
+        to = pl.ds(j, n_dev, stride=seg_count)
+        for p in range(2):
+            for e in range(SEG // LANES):
+                by_brick[p * (SEG // LANES) + e, to, :] = acc[p, j, :, e * LANES:(e + 1) * LANES]
+        by_brick[2 * SEG // LANES, to, :] = mass_acc[j * n_dev:(j + 1) * n_dev]
+
     def pack(b, c):
         at = pl.ds(pl.multiple_of(b * seg_count, seg_count), seg_count)
-        msg[b, :, 0:SEG] = jnp.concatenate([acc[0, at, :], acc[1, at, :]], axis=0).astype(bf16)
-        m = mass_acc[at, :]
+        each = SEG // LANES
+        for e in range(each):
+            both = jnp.concatenate([by_brick[e, at, :], by_brick[each + e, at, :]], axis=0)
+            msg[b, :, e * LANES:(e + 1) * LANES] = both.astype(bf16)
+        m = by_brick[2 * each, at, :]
         hi = m.astype(bf16).astype(f32)
         msg[b, :, SEG:SEG + LANES] = jnp.concatenate([hi, m - hi], axis=0).astype(bf16)
         return c
@@ -380,8 +385,9 @@
     pieces = n_or * halves
     coef = np.arange(k_count)
     shift = np.arange(SHIFTS)
-    index = ((shift % 4)[:, None] * (coef % frame_side - frame_side // 2)[None, :]
-             + (shift // 4)[:, None] * (coef // frame_side)[None, :]) % frame_side
+    shift = shift[:SHIFTS // 2]
+    index = ((shift % 4 - 1.5)[:, None] * (coef % frame_side - frame_side // 2)[None, :]
+             + (shift // 4 - 1.5)[:, None] * (coef // frame_side)[None, :])
     angle = 2 * np.pi * index / frame_side
     cos_tab = jnp.asarray(np.cos(angle), f32)
     sin_tab = jnp.asarray(np.sin(angle), f32)
@@ -401,13 +407,14 @@
             pltpu.VMEM((pieces * rows, width), bf16),
             pltpu.VMEM((pieces * rows, orients), f32),
             pltpu.VMEM((1, orients), f32),
-            pltpu.VMEM((n_dev, seg_count, orients), f32),
+            pltpu.VMEM((seg_count, n_dev, orients), bf16),
             pltpu.VMEM((pieces, pp, LANES), f32),
             pltpu.VMEM((pieces, n_or, 8, LANES), f32),
             pltpu.VMEM((n_dev * seg_count, pieces * rows), bf16),
             pltpu.VMEM((n_or * per, LANES), f32),
             pltpu.VMEM((n_or * per, LANES), f32),
-            pltpu.VMEM((2, n_dev * seg_count, SEG), f32),
+            pltpu.VMEM((2, seg_count, n_dev, SEG), f32),
+            pltpu.VMEM((2 * SEG // LANES + 1, n_dev * seg_count, LANES), f32),
             pltpu.VMEM((n_dev * seg_count, LANES), f32),
             pltpu.VMEM((n_dev, 2 * seg_count, SEG + LANES), bf16),
             pltpu.VMEM((n_dev, 2 * seg_count, SEG + LANES), bf16),

time: 48.3 us -> 46.6 us (0.965)
  Pallas kernels: 47.5 us -> 45.8 us
    pallas_call x1, Pallas kernels: 46.3 us -> 44.5 us  [per_device(): pl.pallas_call(functools.partial(body, (n_or, n_img, n_brick, halves)), o...]
where the time goes in v3:
time: 46.6 us; the launch traced here: 46.4 us
  Pallas kernels  45.8 us (98%)
  between operations  0.64 us (1%)
    pallas_call x1, Pallas kernels, per_device(): pl.pallas_call(functools.partial(body, (n_or, n_img, n_brick, halves)), o...  44.5 us
    pallas_call x1, Pallas kernels, per_device(): pl.pallas_call(hand_out, out_shape=(jax.ShapeDtypeStruct((1, 2, SEG), f32...  1.26 us

profile of v3, /device:TPU:0, one launch (start us, length us, event | category | flops | bytes accessed | tf_op | source)
XLA Modules:
  0.0 46.4 jit_solution(3818812413666515631)
XLA Ops:
  0.6 44.5 %score_and_insert.1.result = f32[3,256]{1,0:T(4,128)} custom-call(bf16[32,4096]{1,0:T(8,128)(2,1)} %images.1, s32[2,512]{1,0:T(2,128)} %bitcast.3, bf16[256,4096]{1,0:T(8,128)(2,1)} %slices_hbm.1, s32[1,8192]{1,0:T(1,128)} %bitcast.2, s32[1,8,256,256]{3,2,1,0:T(8,128)} %interp_hbm.1, f32[8,2048]{1,0:T(8,128)} %constant.4.clone.cos_tab, ...), custom_call_target="tpu_custom_call" | custom-call | tf_op jit(solution)/shard_map/score_and_insert/pallas_call | solution.py:397
  45.2 1.3 %hand_out.1 = (f32[1,2,256]{2,1,0:T(2,128)}, f32[1,256]{1,0:T(1,128)}) custom-call(f32[3,256]{1,0:T(4,128)} %score_and_insert.1.result), custom_call_target="tpu_custom_call" | custom-call | tf_op jit(solution)/shard_map/hand_out/pallas_call | solution.py:435

commit v4 on v3

--- a/solution.py
+++ b/solution.py
@@ -196,28 +196,44 @@
         return pltpu.make_async_remote_copy(stats.at[q, 0], stats.at[q, i], stat_send.at[q, i], stat_recv.at[q, i],
                                             device_id={"orient": (o + i) % n_or}, device_id_type=MESH)
 
+    steps = n_or * halves
+    inner = (o > 0) & (o < n_or - 1)
+
+    def relay(step):
+        t, h = step // halves, step % halves
+        live = (t > 0) & (t < n_or)
+        has_left = live & (o - t >= 0)
+        has_right = live & (o + t < n_or)
+
+        @pl.when(has_left)
+        def _():
+            from_left(t, h).wait_recv()
+
+        @pl.when(has_left & (o < n_or - 1))
+        def _():
+            to_right(t, h).start()
+
+        @pl.when(has_right)
+        def _():
+            from_right(t, h).wait_recv()
+
+        @pl.when(has_right & (o > 0))
+        def _():
+            to_left(t, h).start()
+
     def distance(step, c):
         t, h = step // halves, step % halves
-        has_left = (t > 0) & (o - t >= 0)
-        has_right = (t > 0) & (o + t < n_or)
-
-        @pl.when(has_left)
-        def _():
-            from_left(t, h).wait_recv()
-
-        @pl.when(has_left & (o < n_or - 1))
-        def _():
-            to_right(t, h).start()
-
-        @pl.when(has_right)
-        def _():
-            from_right(t, h).wait_recv()
-
-        @pl.when(has_right & (o > 0))
-        def _():
-            to_left(t, h).start()
 
         def side(d, c):
+            @pl.when((d == 0) | (t > 0))
+            def _():
+                at = jnp.where(t > 0, 2 * step - halves + d, step) + 1
+                ahead = jnp.where(inner, at, jnp.where(d == 0, step, steps))
+
+                @pl.when(ahead < steps)
+                def _():
+                    relay(ahead)
+
             k = o + t * (2 * d - 1)
             live = (k >= 0) & (k < n_or) & ((t > 0) | (d == 0))
 
@@ -227,7 +243,6 @@
             return c
 
         return lax.fori_loop(0, 2, side, c)
-
 
     def collect(step, c):
         k, h = c + step // halves, step % halves
@@ -263,7 +278,6 @@
                 acc[p, j] = got if fresh else acc[p, j] + got
 
     quarter = n_or // 4
-    steps = n_or * halves
     early = (n_or - 1) * halves if quarter else steps
     lax.fori_loop(0, early, distance, 0)
     if quarter:

time: 46.6 us -> 47.1 us (1.011)
  Pallas kernels: 45.8 us -> 46.3 us
    pallas_call x1, Pallas kernels: 44.5 us -> 45 us  [per_device(): pl.pallas_call(functools.partial(body, (n_or, n_img, n_brick, halves)), o...]
where the time goes in v4:
time: 47.1 us; the launch traced here: 46.9 us
  Pallas kernels  46.3 us (98%)
  between operations  0.64 us (1%)
    pallas_call x1, Pallas kernels, per_device(): pl.pallas_call(functools.partial(body, (n_or, n_img, n_brick, halves)), o...  45 us
    pallas_call x1, Pallas kernels, per_device(): pl.pallas_call(hand_out, out_shape=(jax.ShapeDtypeStruct((1, 2, SEG), f32...  1.26 us

profile of v4, /device:TPU:0, one launch (start us, length us, event | category | flops | bytes accessed | tf_op | source)
XLA Modules:
  0.0 46.9 jit_solution(13074229925835593435)
XLA Ops:
  0.6 45.0 %score_and_insert.1.result = f32[3,256]{1,0:T(4,128)} custom-call(bf16[32,4096]{1,0:T(8,128)(2,1)} %images.1, s32[2,512]{1,0:T(2,128)} %bitcast.3, bf16[256,4096]{1,0:T(8,128)(2,1)} %slices_hbm.1, s32[1,8192]{1,0:T(1,128)} %bitcast.2, s32[1,8,256,256]{3,2,1,0:T(8,128)} %interp_hbm.1, f32[8,2048]{1,0:T(8,128)} %constant.4.clone.cos_tab, ...), custom_call_target="tpu_custom_call" | custom-call | tf_op jit(solution)/shard_map/score_and_insert/pallas_call | solution.py:411
  45.7 1.3 %hand_out.1 = (f32[1,2,256]{2,1,0:T(2,128)}, f32[1,256]{1,0:T(1,128)}) custom-call(f32[3,256]{1,0:T(4,128)} %score_and_insert.1.result), custom_call_target="tpu_custom_call" | custom-call | tf_op jit(solution)/shard_map/hand_out/pallas_call | solution.py:449

commit v5 on v4

--- a/solution.py
+++ b/solution.py
@@ -30,7 +30,7 @@
 
 
 def body(cfg, images, offs, slices_hbm, seg_map, interp_hbm, cos_tab, sin_tab, result_out,
-         img_buf, slices, interp, weights, shifted, terms, half_norm, hits, tops, stats, shares, off_a, off_b, acc, by_brick, mass_acc,
+         img_buf, slices, slices_t, interp, weights, shifted, terms, half_norm, hits, tops, stats, shares, off_a, off_b, acc, by_brick, mass_acc,
          msg, inbox, load_sem, send_r, send_l, recv_l, recv_r, stat_send, stat_recv, msg_send, msg_recv):
     n_or, n_img, n_brick, halves = cfg
     n_grp = n_img * n_brick
@@ -129,13 +129,13 @@
     load_slices.wait()
 
     def squares(b, total):
-        block = slices[:, pl.ds(pl.multiple_of(b * LANES, LANES), LANES)].astype(f32)
-        return total + block * block
-
-    norm = lax.fori_loop(0, width // LANES, squares, jnp.zeros((orients, LANES), f32))
-    norm = 0.5 * jnp.sum(norm, axis=1, keepdims=True)
-    diag = lax.broadcasted_iota(jnp.int32, (orients, orients), 0) == lax.broadcasted_iota(jnp.int32, (orients, orients), 1)
-    half_norm[...] = jnp.sum(jnp.where(diag, norm, 0.0), axis=0, keepdims=True)
+        at = pl.ds(pl.multiple_of(b * LANES, LANES), LANES)
+        block = slices[:, at].astype(f32).T
+        slices_t[at, :] = block.astype(bf16)
+        return total + jnp.sum((block * block).reshape(LANES // 8, 8, orients), axis=0)
+
+    norm = lax.fori_loop(0, width // LANES, squares, jnp.zeros((8, orients), f32))
+    half_norm[...] = 0.5 * jnp.sum(norm, axis=0, keepdims=True)
 
     mass_acc[...] = jnp.zeros_like(mass_acc)
 
@@ -179,7 +179,7 @@
 
         lax.fori_loop(0, k_count // LANES, columns, start, unroll=2)
         at = pl.ds(pl.multiple_of(base, rows), rows)
-        got = inv_noise * (nt(shifted[at, :], slices[...]) - half_norm[...])
+        got = inv_noise * (jnp.dot(shifted[at, :], slices_t[...], preferred_element_type=f32) - half_norm[...])
         got = got.reshape(SHIFTS, pp, orients)
         top = jnp.max(jnp.max(got, axis=0), axis=1, keepdims=True)
         term = jnp.exp(got - top[None])
@@ -416,6 +416,7 @@
         scratch_shapes=[
             pltpu.VMEM((n_or, per, width), bf16),
             pltpu.VMEM((orients, width), bf16),
+            pltpu.VMEM((width, orients), bf16),
             pltpu.VMEM((seg_count, SEG, SEG), jnp.int32),
             pltpu.VMEM((seg_count, SEG, 2 * SEG), bf16),
             pltpu.VMEM((pieces * rows, width), bf16),

time: 47.1 us -> 47.1 us (level)
  no operation moved by 1% of the time
where the time goes in v5:
time: 47.1 us; the launch traced here: 46.9 us
  Pallas kernels  46.3 us (98%)
  between operations  0.64 us (1%)
    pallas_call x1, Pallas kernels, per_device(): pl.pallas_call(functools.partial(body, (n_or, n_img, n_brick, halves)), o...  45 us
    pallas_call x1, Pallas kernels, per_device(): pl.pallas_call(hand_out, out_shape=(jax.ShapeDtypeStruct((1, 2, SEG), f32...  1.26 us

profile of v5, /device:TPU:0, one launch (start us, length us, event | category | flops | bytes accessed | tf_op | source)
XLA Modules:
  0.0 46.9 jit_solution(4568012236880798303)
XLA Ops:
  0.6 45.0 %score_and_insert.1.result = f32[3,256]{1,0:T(4,128)} custom-call(bf16[32,4096]{1,0:T(8,128)(2,1)} %images.1, s32[2,512]{1,0:T(2,128)} %bitcast.3, bf16[256,4096]{1,0:T(8,128)(2,1)} %slices_hbm.1, s32[1,8192]{1,0:T(1,128)} %bitcast.2, s32[1,8,256,256]{3,2,1,0:T(8,128)} %interp_hbm.1, f32[8,2048]{1,0:T(8,128)} %constant.4.clone.cos_tab, ...), custom_call_target="tpu_custom_call" | custom-call | tf_op jit(solution)/shard_map/score_and_insert/pallas_call | solution.py:411
  45.6 1.3 %hand_out.1 = (f32[1,2,256]{2,1,0:T(2,128)}, f32[1,256]{1,0:T(1,128)}) custom-call(f32[3,256]{1,0:T(4,128)} %score_and_insert.1.result), custom_call_target="tpu_custom_call" | custom-call | tf_op jit(solution)/shard_map/hand_out/pallas_call | solution.py:450
